TPU v7x, 32 devices: a whole 2x2x4 slice. The times are simulated.
32 devices in a mesh: expert: 4 (over y, x), tensor: 8 (over z, core).
Axes of the slice: x: 2, y: 2, z: 4, core: 2. Of those that a mesh axis runs over, the one named last changes fastest.
Arguments:
- tokens: bfloat16 [512, 6144], P('expert'), may hold values from -6 to 6
- routes: int32 [512, 4], P('expert'), may hold values from 0 to 15, all different within a row; in each aligned block of 128 rows (0 to 127, 128 to 255, ...) at most 40 rows name the same one
- gates: float32 [512, 4], P('expert'), may hold values from 0.05 to 1
- gate_proj: bfloat16 [4, 10752, 6144], P('expert', 'tensor'), may hold values from -0.078125 to 0.078125
- up_proj: bfloat16 [4, 10752, 6144], P('expert', 'tensor'), may hold values from -0.078125 to 0.078125
- down_proj: bfloat16 [4, 6144, 10752], P('expert', 'tensor'), may hold values from -0.0625 to 0.0625
Outputs:
- combined: bfloat16 [512, 6144], P('expert', 'tensor')
Inputs may be any that keep to these rules, and one draw needn't show every extreme that they name: `routes`: the ids of one row are distinct. In each aligned block of 128 rows no id is named by more than 40 rows, a bound that some block reaches.
All inputs are finite; a program needn't handle non-finite values.
Results may differ from a plain program's by a relative error of at most 0.0057.
Values may be sent and summed in bfloat16 or wider, within the bound.
A program may use at most 128 MiB of HBM per device.

v0:
```python
import jax
import jax.numpy as jnp
from jax import lax
from jax.sharding import PartitionSpec as P

WIN = 4
CAP = 40


def slot_tables(route_block, gate_block):
    row_count = route_block.shape[0]
    experts = jnp.arange(WIN, dtype=jnp.int32)
    hits = route_block[None, :, :] == experts[:, None, None]
    chosen = jnp.any(hits, axis=2)
    position = jnp.cumsum(chosen.astype(jnp.int32), axis=1) - 1
    slots = jnp.arange(CAP, dtype=jnp.int32)
    match = chosen[:, None, :] & (position[:, None, :] == slots[None, :, None])
    row_ids = jnp.arange(row_count, dtype=jnp.int32)
    row_index = jnp.sum(jnp.where(match, row_ids[None, None, :], 0), axis=2)
    filled = jnp.any(match, axis=2)
    weight = jnp.sum(
        jnp.where(hits, gate_block[None, :, :], jnp.zeros((), gate_block.dtype)), axis=2
    )
    return (position, row_index, filled, weight)


def contract_last(left, right):
    return lax.dot_general(
        left, right, (((1,), (1,)), ((), ())), preferred_element_type=jnp.float32
    )


def body(tokens, routes, gates, gate_proj, up_proj, down_proj):
    groups = lax.axis_size("expert")
    split = groups // WIN
    width = tokens.shape[1]
    w_gate = gate_proj[0]
    w_up = up_proj[0]
    w_down = down_proj[0]
    position, row_index, filled, weight = slot_tables(routes, gates)
    picked = jnp.take(tokens, row_index, axis=0)
    picked = jnp.where(filled[:, :, None], picked, jnp.zeros((), tokens.dtype))
    outgoing = jnp.repeat(picked, split, axis=0)
    slot_rows = groups * CAP
    arrived = lax.all_to_all(outgoing, "expert", split_axis=0, concat_axis=0, tiled=True)
    flat_rows = arrived.reshape(slot_rows, width)
    gate_act = contract_last(flat_rows, w_gate)
    up_act = contract_last(flat_rows, w_up)
    hidden = (jax.nn.silu(gate_act) * up_act).astype(jnp.bfloat16)
    partial_value = contract_last(lax.all_gather(hidden, "tensor", axis=1, tiled=True), w_down)
    partial_value = partial_value.astype(jnp.bfloat16).reshape(groups, CAP, w_down.shape[0])
    returned = lax.all_to_all(partial_value, "expert", split_axis=0, concat_axis=0, tiled=True)
    expert_out = returned.astype(jnp.float32).reshape(WIN, split, CAP, w_down.shape[0]).sum(axis=1)
    flat_sum = expert_out.reshape(WIN * CAP, w_down.shape[0])
    offsets = jnp.arange(WIN, dtype=jnp.int32)[:, None] * CAP
    index = offsets + jnp.clip(position, 0, CAP - 1)
    values = jnp.take(flat_sum, index, axis=0)
    return jnp.sum(values * weight[:, :, None], axis=0).astype(jnp.bfloat16)


def solution(mesh):
    in_specs = (
        P("expert", None),
        P("expert", None),
        P("expert", None),
        P("expert", "tensor", None),
        P("expert", "tensor", None),
        P("expert", "tensor", None),
    )
    out_specs = P("expert", "tensor")
    return jax.shard_map(body, mesh=mesh, in_specs=in_specs, out_specs=out_specs, check_vma=False)
```

profile of v0, /device:TPU:0, one launch (start us, length us, event | category | flops | bytes accessed | tf_op | source)
XLA Modules:
  0.0 148.9 jit_solution(7978255805247164099)
XLA Ops:
  6.5 0.8 fusion.20
  7.4 0.3 reduce_window_sum.11
  7.7 0.1 select_reduce_fusion
  7.9 0.1 fusion.19
  8.0 0.1 reshape.118
  8.1 1.7 %gather_fusion = bf16[160,6144]{1,0:T(8,128)(2,1)S(1)} fusion(bf16[128,6144]{1,0:T(8,128)(2,1)S(1)} %copy-done, s32[1024]{0:T(1024)S(1)} %pad_clamp_fusion.1), kind=kCustom, calls=%fused_computation | custom fusion | bytes 3932800 | tf_op jit(solution)/shard_map/jit(_take)/gather | solution.py:41
  9.8 0.3 select_select_fusion
  10.1 28.9 %all_to_all.10 = bf16[4,40,6144]{2,1,0:T(8,128)(2,1)S(1)} all-to-all(bf16[4,40,6144]{2,1,0:T(8,128)(2,1)S(1)} %select_select_fusion), channel_id=1, replica_groups=mesh['expert'=4,'tensor'=8] {'expert'}, dimensions={0} | all-to-all | bytes 3932160 | tf_op jit(solution)/shard_map/all_to_all | solution.py:45
  39.1 9.3 %fusion.4 = f32[160,1344]{1,0:T(8,128)S(1)} fusion(bf16[160,6144]{1,0:T(8,128)(2,1)S(1)} %bitcast.45, bf16[1,1344,6144]{2,1,0:T(8,128)(2,1)} %param.9), kind=kOutput, calls=%fused_computation.6 | convolution fusion | flops 2642411520 | bytes 19341312 | tf_op jit(solution)/shard_map/dot_general | solution.py:28
  48.4 0.0 copy-start.2
  48.4 0.0 copy-start.3
  48.4 12.3 %fusion.12 = bf16[1,1344,160]{1,2,0:T(8,128)(2,1)} fusion(bf16[160,6144]{1,0:T(8,128)(2,1)S(1)} %bitcast.46, bf16[1,1344,6144]{2,1,0:T(8,128)(2,1)} %param.10, f32[160,1344]{1,0:T(8,128)S(1)} %fusion.4), kind=kOutput, calls=%fused_computation.10 | convolution fusion | flops 2643701760 | bytes 19771392 | tf_op jit(solution)/shard_map/dot_general | solution.py:28
  60.7 0.0 all-gather.3.cloned.1.call-update
  60.7 0.1 fusion.21
  60.8 41.8 %all-gather.3.cloned.1.call-done = bf16[8,1344,160]{1,2,0:T(8,128)(2,1)} async-done(((bf16[1,1344,160]{1,2,0:T(8,128)(2,1)}), bf16[8,1344,160]{1,2,0:T(8,128)(2,1)}) %all-gather.3.cloned.1.call-update) | async-done | bytes 3440656 | tf_op jit(solution)/shard_map/all_gather | solution.py:50
  102.6 5.0 %copy.15 = bf16[8,1344,160]{1,0,2:T(8,128)(2,1)} copy(bf16[8,1344,160]{1,2,0:T(8,128)(2,1)} %all-gather.3.cloned.1.call-done) | data formatting | bytes 6881280 | tf_op jit(solution)/shard_map/all_gather | solution.py:50
  107.6 7.2 %reshape.135 = bf16[10752,160]{0,1:T(8,128)(2,1)} reshape(bf16[8,1344,160]{1,0,2:T(8,128)(2,1)} %copy.15) | data formatting | bytes 6881280
  114.8 12.9 %fusion.15 = bf16[160,768]{1,0:T(8,128)(2,1)} fusion(bf16[10752,160]{0,1:T(8,128)(2,1)} %reshape.135, bf16[1,768,10752]{2,1,0:T(8,128)(2,1)} %param.11), kind=kOutput, calls=%fused_computation.13 | convolution fusion | flops 2642534400 | bytes 20201472 | tf_op jit(solution)/shard_map/dot_general | solution.py:28
  127.7 3.6 %all-to-all-start.1 = ((bf16[4,40,768]{2,1,0:T(8,128)(2,1)}), bf16[4,40,768]{2,1,0:T(8,128)(2,1)S(1)}, u32[]{:S(2)}, u32[]{:S(2)}) async-start(bf16[4,40,768]{2,1,0:T(8,128)(2,1)} %bitcast.8), calls=%async_computation.1 | async-start | bytes 491520 | tf_op jit(solution)/shard_map/all_to_all | solution.py:52
  131.3 0.1 compare_and_fusion.1
  131.4 5.6 %all-to-all-done.1 = bf16[4,40,768]{2,1,0:T(8,128)(2,1)S(1)} async-done(((bf16[4,40,768]{2,1,0:T(8,128)(2,1)}), bf16[4,40,768]{2,1,0:T(8,128)(2,1)S(1)}, u32[]{:S(2)}, u32[]{:S(2)}) %all-to-all-start.1) | async-done | bytes 245792 | tf_op jit(solution)/shard_map/all_to_all | solution.py:52
  137.0 0.1 bitcast_convert_fusion
  137.0 2.6 %gather_fusion.1 = f32[512,768]{1,0:T(8,128)} fusion(f32[160,768]{1,0:T(8,128)S(1)} %bitcast_convert_fusion, s32[1024]{0:T(1024)S(1)} %pad_clamp_fusion), kind=kCustom, calls=%fused_computation.1 | custom fusion | bytes 3147776 | tf_op jit(solution)/shard_map/jit(_take)/gather | solution.py:57
  139.6 2.4 %multiply_reduce_fusion = bf16[128,768]{1,0:T(8,128)(2,1)} fusion(f32[4,128,768]{2,1,0:T(8,128)} %bitcast.44, f32[4,128]{1,0:T(4,128)S(1)} %select_reduce_fusion.1, pred[4,128]{1,0:T(4,128)(4,1)S(1)} %compare_and_fusion.1), kind=kLoop, calls=%fused_computation.12 | loop fusion | flops 1081344 | bytes 1772032 | tf_op jit(solution)/shard_map/reduce_sum | solution.py:58
  (15 shorter events, 0.1 us)
Async XLA Ops:
  6.5 1.6 %copy-start = (bf16[128,6144]{1,0:T(8,128)(2,1)S(1)}, bf16[128,6144]{1,0:T(8,128)(2,1)}, u32[]{:S(2)}) copy-start(bf16[128,6144]{1,0:T(8,128)(2,1)} %param.6) | copy-start | bytes 4718596
  6.5 96.1 %all-gather.3.cloned.1.call-start = ((), (), s32[]{:S(2)}) async-start(), calls=%async_computation.2 | async-start | bytes 4055040 | tf_op jit(solution)/shard_map/all_gather | solution.py:50
  48.4 12.4 %copy-start.2 = (s32[128,4]{0,1:T(4,128)S(1)}, s32[128,4]{0,1:T(4,128)}, u32[]{:S(2)}) copy-start(s32[128,4]{0,1:T(4,128)} %param.7) | copy-start | bytes 6148
  48.4 12.4 %copy-start.3 = (f32[128,4]{0,1:T(4,128)S(1)}, f32[128,4]{0,1:T(4,128)}, u32[]{:S(2)}) copy-start(f32[128,4]{0,1:T(4,128)} %param.8) | copy-start | bytes 6148
  127.7 9.3 %all-to-all-start.1 = ((bf16[4,40,768]{2,1,0:T(8,128)(2,1)}), bf16[4,40,768]{2,1,0:T(8,128)(2,1)S(1)}, u32[]{:S(2)}, u32[]{:S(2)}) async-start(bf16[4,40,768]{2,1,0:T(8,128)(2,1)} %bitcast.8), calls=%async_computation.1 | async-start | bytes 491520 | tf_op jit(solution)/shard_map/all_to_all | solution.py:52
  137.0 5.0 %copy-start.1 = (bf16[128,6144]{1,0:T(8,128)(2,1)S(1)}, bf16[128,6144]{1,0:T(8,128)(2,1)}, u32[]{:S(2)}) copy-start(bf16[128,6144]{1,0:T(8,128)(2,1)} %param.6) | copy-start | bytes 4718596
Sparse Core Ops, SparseCore 0:
  60.8 41.7 all-gather.2
where the time goes:
time: 149 us
  waiting for transfers between devices  47.4 us (32%)
  matrix products  34.5 us (23%)
  blocking collectives  28.9 us (19%)
  local copies, waits for them, and re-layouts  16.6 us (11%)
  between operations  13.5 us (9%)
  other arithmetic  4.34 us (3%)
  starting transfers between devices  3.65 us (2%)
    all_gather x1, waiting for transfers between devices, body(): lax.all_gather(hidden, 'tensor', axis=1, tiled=True)  41.8 us
    dot_general x3, matrix products, contract_last(): lax.dot_general(left, right, (((1,), (1,)), ((), ())), preferred_element_...  34.5 us
    all_to_all x1, blocking collectives, body(): lax.all_to_all(outgoing, 'expert', split_axis=0, concat_axis=0, tiled=True)  28.9 us
    unnamed x9, local copies, waits for them, and re-layouts  7.2 us
    all_to_all x1, waiting for transfers between devices, body(): lax.all_to_all(partial_value, 'expert', split_axis=0, concat_axis=0, tile...  5.56 us
    all_gather x1, local copies, waits for them, and re-layouts, body(): lax.all_gather(hidden, 'tensor', axis=1, tiled=True)  4.95 us
    all_to_all x1, starting transfers between devices, body(): lax.all_to_all(partial_value, 'expert', split_axis=0, concat_axis=0, tile...  3.65 us
  transfers between devices with their start and end apart: 2, of which 2 were waited for; matrix products, arithmetic and copies ran while one was open for 0% of the time, Pallas kernels for 0%

commit v1 on v0

--- a/solution.py
+++ b/solution.py
@@ -1,10 +1,14 @@
+import functools
 import jax
 import jax.numpy as jnp
 from jax import lax
+from jax.experimental import pallas as pl
+from jax.experimental.pallas import tpu as pltpu
 from jax.sharding import PartitionSpec as P
 
 WIN = 4
 CAP = 40
+MESH = pl.DeviceIdType.MESH
 
 
 def slot_tables(route_block, gate_block):
@@ -30,7 +34,7 @@
     )
 
 
-def body(tokens, routes, gates, gate_proj, up_proj, down_proj):
+def plain_body(tokens, routes, gates, gate_proj, up_proj, down_proj):
     groups = lax.axis_size("expert")
     split = groups // WIN
     width = tokens.shape[1]
@@ -58,6 +62,349 @@
     return jnp.sum(values * weight[:, :, None], axis=0).astype(jnp.bfloat16)
 
 
+CUTS = (0, 32, 112, 160)
+CHUNK = 256
+
+
+def kernel(cfg, tok_h, rou_h, gat_h, wg_h, wu_h, wd_h, out_ref,
+           tok, rou, gat, wg, wu, wd, sbuf, xr, xa, xb, xc, hid, carry, acc, pbuf, ret, wmat,
+           in_sem, w_sem, d_sem, ds_send, ds_recv, fw_send, fw_recv,
+           up_send, dn_send, sb_send, ag_recv, rt_send, rt_recv):
+    depth, units, feats, rows = cfg
+    chips = 4
+    quarter = depth // 4
+    pad_units = wg.shape[0]
+    half_pad = pad_units - units
+    me = lax.axis_index("expert")
+    t = lax.axis_index("tensor")
+    z = t // 2
+    c = t % 2
+    x = me % 2
+    y = me // 2
+    sib = t + 1 - 2 * c
+    rel = [me, y * 2 + (1 - x), (1 - y) * 2 + x, (1 - y) * 2 + (1 - x)]
+
+    small = [pltpu.make_async_copy(rou_h, rou, in_sem.at[0]),
+             pltpu.make_async_copy(gat_h, gat, in_sem.at[1]),
+             pltpu.make_async_copy(tok_h, tok, in_sem.at[2])]
+    for copy in small:
+        copy.start()
+    spans = [(k, min(CHUNK, units - k)) for k in range(0, units, CHUNK)]
+    loads = []
+    for k, (start, size) in enumerate(spans):
+        dst = pl.multiple_of(start + half_pad * c, half_pad)
+        loads.append([
+            pltpu.make_async_copy(wg_h.at[0, pl.ds(start, size), :], wg.at[pl.ds(dst, size), :], w_sem.at[0, k]),
+            pltpu.make_async_copy(wu_h.at[0, pl.ds(start, size), :], wu.at[pl.ds(dst, size), :], w_sem.at[1, k])])
+    for pair in loads:
+        for copy in pair:
+            copy.start()
+    wd_load = pltpu.make_async_copy(wd_h.at[0], wd, d_sem)
+    wd_load.start()
+    gap = pl.multiple_of((1 - c) * units, half_pad)
+    wg[pl.ds(gap, half_pad), :] = jnp.zeros((half_pad, depth), wg.dtype)
+    wu[pl.ds(gap, half_pad), :] = jnp.zeros((half_pad, depth), wu.dtype)
+
+    barrier = pltpu.get_barrier_semaphore()
+    for r in (1, 2, 3):
+        pl.semaphore_signal(barrier, inc=1, device_id=(rel[r], t), device_id_type=MESH)
+    pl.semaphore_signal(barrier, inc=1, device_id=(me, sib), device_id_type=MESH)
+
+    @pl.when(z < chips - 1)
+    def _():
+        pl.semaphore_signal(barrier, inc=1, device_id=(me, t + 2), device_id_type=MESH)
+
+    @pl.when(z > 0)
+    def _():
+        pl.semaphore_signal(barrier, inc=1, device_id=(me, t - 2), device_id_type=MESH)
+
+    small[0].wait()
+    small[1].wait()
+    lane = lax.broadcasted_iota(jnp.int32, (rows, 256), 1)
+    group = (lane >= CAP).astype(jnp.int32) + (lane >= 2 * CAP).astype(jnp.int32) + (lane >= 3 * CAP).astype(jnp.int32)
+    named = jnp.where(group == 0, rel[0], jnp.where(group == 1, rel[1], jnp.where(group == 2, rel[2], rel[3])))
+    named = jnp.where(lane >= 4 * CAP, -1, named)
+    slot = lane - CAP * group
+    routes = rou[...]
+    gates = gat[...]
+    chosen = jnp.zeros((rows, 256), jnp.float32)
+    weight = jnp.zeros((rows, 256), jnp.float32)
+    for k in range(routes.shape[1]):
+        hit = routes[:, k:k + 1] == named
+        chosen = jnp.where(hit, 1.0, chosen)
+        weight = jnp.where(hit, gates[:, k:k + 1], weight)
+    lower = (lax.broadcasted_iota(jnp.int32, (rows, rows), 0) >= lax.broadcasted_iota(jnp.int32, (rows, rows), 1))
+    lower = jnp.where(lower, 1.0, 0.0).astype(jnp.bfloat16)
+    count = jnp.dot(lower, chosen.astype(jnp.bfloat16), preferred_element_type=jnp.float32)
+    match = jnp.where((chosen > 0.5) & (count == (slot + 1).astype(jnp.float32)), 1.0, 0.0)
+    wfull = weight * match
+    whigh = wfull.astype(jnp.bfloat16)
+    wmat[0] = whigh
+    wmat[1] = (wfull - whigh.astype(jnp.float32)).astype(jnp.bfloat16)
+    pick = match.T.astype(jnp.bfloat16)[:4 * CAP]
+
+    small[2].wait()
+    for r in (1, 2, 3):
+        pass
+    for piece in range(0, quarter, 512):
+        vals = []
+        for q in range(2):
+            col = pl.multiple_of(c * 2 * quarter + q * quarter + piece, 128)
+            vals.append(jnp.dot(pick, tok[:, pl.ds(col, 512)], preferred_element_type=jnp.float32))
+        for r in (1, 2, 3):
+            both = jnp.concatenate([v[r * CAP:(r + 1) * CAP] for v in vals], axis=0)
+            sbuf[r - 1, :, piece:piece + 512] = both.astype(jnp.bfloat16)
+    pl.semaphore_wait(barrier, 4 + (z > 0).astype(jnp.int32) + (z < chips - 1).astype(jnp.int32))
+    sends = []
+    for r in (1, 2, 3):
+        copy = pltpu.make_async_remote_copy(
+            src_ref=sbuf.at[r - 1], dst_ref=xr.at[c, r - 1], send_sem=ds_send.at[r - 1],
+            recv_sem=ds_recv.at[r - 1], device_id=(rel[r], t), device_id_type=MESH)
+        copy.start()
+        sends.append(copy)
+    own = jnp.concatenate([pick[:CAP].astype(jnp.float32), jnp.zeros((8, rows), jnp.float32)], axis=0).astype(jnp.bfloat16)
+    for col in range(0, depth, 512):
+        xa[:, col:col + 512] = jnp.dot(own, tok[:, col:col + 512], preferred_element_type=jnp.float32).astype(jnp.bfloat16)
+
+    forwards = []
+
+    def forward(r):
+        sends[r - 1].wait_recv()
+        copy = pltpu.make_async_remote_copy(
+            src_ref=xr.at[c, r - 1], dst_ref=xr.at[c, r - 1], send_sem=fw_send.at[r - 1],
+            recv_sem=fw_recv.at[r - 1], device_id=(me, sib), device_id_type=MESH)
+        copy.start()
+        forwards.append(copy)
+
+    def sibling_in(r):
+        pltpu.make_async_remote_copy(
+            src_ref=xr.at[1 - c, r - 1], dst_ref=xr.at[1 - c, r - 1], send_sem=fw_send.at[r - 1],
+            recv_sem=fw_recv.at[r - 1], device_id=(me, sib), device_id_type=MESH).wait_recv()
+
+    def unpack(half, q, r, piece):
+        return xr[half, r - 1, :, piece:piece + 512].astype(jnp.float32)[q * CAP:(q + 1) * CAP]
+
+    groups = [(0, 512), (512, 512), (1024, pad_units - 1024)]
+    pieces = [(p, g) for p in range(3) for g in range(3)]
+    n_pieces = len(pieces)
+
+    def window(shard, n):
+        p, g = pieces[n]
+        return hid.at[shard, pl.ds(CUTS[p], CUTS[p + 1] - CUTS[p]), pl.ds(groups[g][0], groups[g][1])]
+
+    def hop(shard, n, sem, dev):
+        return pltpu.make_async_remote_copy(
+            src_ref=window(shard, n), dst_ref=window(shard, n), send_sem=sem,
+            recv_sem=ag_recv.at[shard, n], device_id=(me, dev), device_id_type=MESH)
+
+    def push(shard, dist, n, do_up, do_dn):
+        if do_up:
+            @pl.when(z < chips - 1)
+            def _():
+                hop(shard, n, up_send.at[dist, n], t + 2).start()
+        if do_dn:
+            @pl.when(z > 0)
+            def _():
+                hop(shard, n, dn_send.at[dist, n], t - 2).start()
+
+    def drain(shard, dist, n, do_up, do_dn):
+        if do_up:
+            @pl.when(z < chips - 1)
+            def _():
+                hop(shard, n, up_send.at[dist, n], t + 2).wait_send()
+        if do_dn:
+            @pl.when(z > 0)
+            def _():
+                hop(shard, n, dn_send.at[dist, n], t - 2).wait_send()
+
+    def relay(dist, n):
+        @pl.when(z >= dist)
+        def _():
+            shard = t - 2 * dist
+            hop(shard, n, up_send.at[dist, n], t).wait_recv()
+            push(shard, dist, n, dist < chips - 1, False)
+            hop(shard, n, sb_send.at[0, dist, n], sib).start()
+
+        @pl.when(z + dist <= chips - 1)
+        def _():
+            shard = t + 2 * dist
+            hop(shard, n, dn_send.at[dist, n], t).wait_recv()
+            push(shard, dist, n, False, dist < chips - 1)
+            hop(shard, n, sb_send.at[1, dist, n], sib).start()
+
+    xs = (xa, xb, xc)
+
+    def compute(p, g):
+        start, size = groups[g]
+        for col in range(start, start + size, CHUNK):
+            width = min(CHUNK, start + size - col)
+            if p == 0:
+                for copy in loads[col // CHUNK]:
+                    copy.wait()
+            left = xs[p][...]
+            ga = contract_last(left, wg[col:col + width, :])
+            ua = contract_last(left, wu[col:col + width, :])
+            h = ga / (1.0 + jnp.exp(-ga)) * ua
+            if p == 0:
+                full = h[:32]
+                carry[0, :, col:col + width] = h[32:40]
+            elif p == 1:
+                full = jnp.concatenate([carry[0, :, col:col + width], h[:72]], axis=0)
+                carry[1, :, col:col + width] = h[72:80]
+            else:
+                full = jnp.concatenate([carry[1, :, col:col + width], h[:40]], axis=0)
+            hid[t, CUTS[p]:CUTS[p + 1], col:col + width] = full.astype(jnp.bfloat16)
+
+    def stage(n):
+        if n < n_pieces:
+            p, g = pieces[n]
+            if g == 0 and p == 1:
+                sibling_in(1)
+                sibling_in(2)
+                for half in range(2):
+                    for q in range(2):
+                        for piece in range(0, quarter, 512):
+                            col = half * 2 * quarter + q * quarter + piece
+                            both = jnp.concatenate([unpack(half, q, 1, piece), unpack(half, q, 2, piece)], axis=0)
+                            xb[:, col:col + 512] = both.astype(jnp.bfloat16)
+            if g == 0 and p == 2:
+                sibling_in(3)
+                for half in range(2):
+                    for q in range(2):
+                        for piece in range(0, quarter, 512):
+                            col = half * 2 * quarter + q * quarter + piece
+                            both = jnp.concatenate([unpack(half, q, 3, piece), jnp.zeros((8, 512), jnp.float32)], axis=0)
+                            xc[:, col:col + 512] = both.astype(jnp.bfloat16)
+            compute(p, g)
+            push(t, 0, n, True, True)
+            hop(t, n, sb_send.at[0, 0, n], sib).start()
+            if (p, g) == (0, 2):
+                forward(1)
+                forward(2)
+            if (p, g) == (1, 1):
+                forward(3)
+        for dist in (1, 2, 3):
+            if 0 <= n - dist < n_pieces:
+                relay(dist, n - dist)
+
+    for n in range(n_pieces):
+        stage(n)
+
+    def down(src, first):
+        for q in range(2):
+            shard = src * 2 + q
+
+            @pl.when(q != c)
+            def _():
+                for n in range(n_pieces):
+                    hop(shard, n, sb_send.at[0, 0, n], sib).wait_recv()
+            off = pl.multiple_of(src * 2 * units + q * (units - half_pad), 128)
+            for col in range(0, feats, CHUNK):
+                part = contract_last(hid[shard], wd[col:col + CHUNK, pl.ds(off, pad_units)])
+                if first and q == 0:
+                    acc[:, col:col + CHUNK] = part
+                else:
+                    acc[:, col:col + CHUNK] += part
+
+    wd_load.wait()
+    down(z, True)
+    low = 1 - z // 2
+    for k in (1, 2, 3):
+        stage(n_pieces + k - 1)
+        up_src = k - (k <= z).astype(jnp.int32)
+        dn_src = 3 - (k - (k <= 3 - z).astype(jnp.int32))
+        down(low * up_src + (1 - low) * dn_src, False)
+
+    half_f = feats // 2
+    back = []
+    for r in (3, 1, 2, 0):
+        block = acc[r * CAP:(r + 1) * CAP, :]
+        packed = jnp.concatenate([block[:, :half_f], block[:, half_f:]], axis=0).astype(jnp.bfloat16)
+        if r == 0:
+            ret[0] = packed
+        else:
+            pbuf[r - 1] = packed
+            copy = pltpu.make_async_remote_copy(
+                src_ref=pbuf.at[r - 1], dst_ref=ret.at[r], send_sem=rt_send.at[r - 1],
+                recv_sem=rt_recv.at[r - 1], device_id=(rel[r], t), device_id_type=MESH)
+            copy.start()
+            back.append(copy)
+    for copy in sends + forwards:
+        copy.wait_send()
+    for n in range(n_pieces):
+        drain(t, 0, n, True, True)
+        hop(t, n, sb_send.at[0, 0, n], sib).wait_send()
+        for dist in (1, 2, 3):
+            @pl.when(z >= dist)
+            def _():
+                drain(t - 2 * dist, dist, n, dist < chips - 1, False)
+                hop(t - 2 * dist, n, sb_send.at[0, dist, n], sib).wait_send()
+
+            @pl.when(z + dist <= chips - 1)
+            def _():
+                drain(t + 2 * dist, dist, n, False, dist < chips - 1)
+                hop(t + 2 * dist, n, sb_send.at[1, dist, n], sib).wait_send()
+    for copy in back:
+        copy.wait()
+    blocks = [ret[r].astype(jnp.float32) for r in range(4)]
+    zero = jnp.zeros((256 - 4 * CAP, half_f), jnp.float32)
+    for q in range(2):
+        stack = jnp.concatenate([b[q * CAP:(q + 1) * CAP] for b in blocks] + [zero], axis=0).astype(jnp.bfloat16)
+        total = jnp.dot(wmat[0], stack, preferred_element_type=jnp.float32)
+        total += jnp.dot(wmat[1], stack, preferred_element_type=jnp.float32)
+        out_ref[:, q * half_f:(q + 1) * half_f] = total.astype(jnp.bfloat16)
+
+
+def fast_body(tokens, routes, gates, gate_proj, up_proj, down_proj):
+    rows, depth = tokens.shape
+    units = gate_proj.shape[1]
+    feats = down_proj.shape[1]
+    pad_units = -(-units // 128) * 128
+    bf = jnp.bfloat16
+    dma = pltpu.SemaphoreType.DMA
+    spans = -(-units // CHUNK)
+    any_spec = pl.BlockSpec(memory_space=pl.ANY)
+    return pl.pallas_call(
+        functools.partial(kernel, (depth, units, feats, rows)),
+        out_shape=jax.ShapeDtypeStruct((rows, feats), bf),
+        in_specs=[any_spec] * 6,
+        out_specs=pl.BlockSpec(memory_space=pltpu.VMEM),
+        scratch_shapes=[
+            pltpu.VMEM((rows, depth), bf),
+            pltpu.VMEM(routes.shape, jnp.int32),
+            pltpu.VMEM(gates.shape, jnp.float32),
+            pltpu.VMEM((pad_units, depth), bf),
+            pltpu.VMEM((pad_units, depth), bf),
+            pltpu.VMEM((feats, down_proj.shape[2]), bf),
+            pltpu.VMEM((3, 2 * CAP, depth // 4), bf),
+            pltpu.VMEM((2, 3, 2 * CAP, depth // 4), bf),
+            pltpu.VMEM((48, depth), bf),
+            pltpu.VMEM((80, depth), bf),
+            pltpu.VMEM((48, depth), bf),
+            pltpu.VMEM((8, 4 * CAP, pad_units), bf),
+            pltpu.VMEM((2, 8, pad_units), jnp.float32),
+            pltpu.VMEM((4 * CAP, feats), jnp.float32),
+            pltpu.VMEM((3, 2 * CAP, feats // 2), bf),
+            pltpu.VMEM((4, 2 * CAP, feats // 2), bf),
+            pltpu.VMEM((2, rows, 256), bf),
+            dma((3,)), dma((2, spans)), dma,
+            dma((3,)), dma((3,)), dma((3,)), dma((3,)),
+            dma((4, 9)), dma((4, 9)), dma((2, 4, 9)), dma((8, 9)),
+            dma((3,)), dma((3,)),
+        ],
+        compiler_params=pltpu.CompilerParams(
+            collective_id=0, has_side_effects=True, vmem_limit_bytes=67000000),
+        cost_estimate=pl.CostEstimate(
+            flops=2 * 4 * CAP * 3 * units * depth, transcendentals=4 * CAP * units,
+            bytes_accessed=3 * 2 * units * depth),
+        name="moe_step",
+    )(tokens, routes, gates, gate_proj, up_proj, down_proj)
+
+
+def tiles(mesh):
+    return mesh.shape["expert"] == WIN and mesh.shape["tensor"] == 8
+
+
 def solution(mesh):
     in_specs = (
         P("expert", None),
@@ -68,4 +415,5 @@
         P("expert", "tensor", None),
     )
     out_specs = P("expert", "tensor")
+    body = fast_body if tiles(mesh) else plain_body
     return jax.shard_map(body, mesh=mesh, in_specs=in_specs, out_specs=out_specs, check_vma=False)

time: 149 us -> 79.1 us (0.53)
  Pallas kernels: 0 us -> 74.5 us
  waiting for transfers between devices: 47.4 us -> 0 us
  matrix products: 34.5 us -> 0 us
  blocking collectives: 28.9 us -> 0 us
  between operations: 13.5 us -> 0.01 us
  local copies, waits for them, and re-layouts: 16.6 us -> 4.44 us
  other arithmetic: 4.34 us -> 0 us
  starting transfers between devices: 3.65 us -> 0 us
    pallas_call x0 -> x1, Pallas kernels: none -> 74.5 us  [fast_body(): pl.pallas_call(functools.partial(kernel, (depth, units, feats, rows)), ou...]
    all_gather x1 -> x0, waiting for transfers between devices: 41.8 us -> none  [body(): lax.all_gather(hidden, 'tensor', axis=1, tiled=True)]
    dot_general x3 -> x0, matrix products: 34.5 us -> none  [contract_last(): lax.dot_general(left, right, (((1,), (1,)), ((), ())), preferred_element_...]
    all_to_all x1 -> x0, blocking collectives: 28.9 us -> none  [body(): lax.all_to_all(outgoing, 'expert', split_axis=0, concat_axis=0, tiled=True)]
    all_to_all x1 -> x0, waiting for transfers between devices: 5.56 us -> none  [body(): lax.all_to_all(partial_value, 'expert', split_axis=0, concat_axis=0, tile...]
    all_gather x1 -> x0, local copies, waits for them, and re-layouts: 4.95 us -> none  [body(): lax.all_gather(hidden, 'tensor', axis=1, tiled=True)]
    gather x2 -> x0, local copies, waits for them, and re-layouts: 4.35 us -> none  [the longest x1 2.62 us: body(): values = jnp.take(flat_sum, index, axis=0)]
    all_to_all x1 -> x0, starting transfers between devices: 3.65 us -> none  [body(): lax.all_to_all(partial_value, 'expert', split_axis=0, concat_axis=0, tile...]
  transfers between devices with their start and end apart: 2 -> 0, of which waited for: 2 -> 0; matrix products, arithmetic and copies ran while one was open for 0% -> 0% of each run, Pallas kernels for 0% -> 0%
where the time goes in v1:
time: 79.1 us; the launch traced here: 79 us
  Pallas kernels  74.5 us (94%)
  local copies, waits for them, and re-layouts  4.44 us (6%)
    pallas_call x1, Pallas kernels, fast_body(): pl.pallas_call(functools.partial(kernel, (depth, units, feats, rows)), ou...  74.5 us
    unnamed x3, local copies, waits for them, and re-layouts  4.44 us

profile of v1, /device:TPU:0, one launch (start us, length us, event | category | flops | bytes accessed | tf_op | source)
XLA Modules:
  0.0 79.0 jit_solution(16036456788268016668)
XLA Ops:
  0.0 1.4 %copy.7.rou_h = s32[128,4]{1,0:T(8,128)} copy(s32[128,4]{0,1:T(4,128)} %param.7) | data formatting | bytes 4096 | tf_op args[1]
  1.4 1.4 %copy.8.gat_h = f32[128,4]{1,0:T(8,128)} copy(f32[128,4]{0,1:T(4,128)} %param.8) | data formatting | bytes 4096 | tf_op args[2]
  2.8 74.5 %moe_step.1 = bf16[128,768]{1,0:T(8,128)(2,1)} custom-call(bf16[128,6144]{1,0:T(8,128)(2,1)} %tok_h.1, s32[128,4]{1,0:T(8,128)} %copy.7.rou_h, f32[128,4]{1,0:T(8,128)} %copy.8.gat_h, bf16[1,1344,6144]{2,1,0:T(8,128)(2,1)} %wg_h.1, bf16[1,1344,6144]{2,1,0:T(8,128)(2,1)} %wu_h.1, bf16[1,768,10752]{2,1,0:T(8,128)(2,1)} %wd_h.1), custom_call_target="tpu_custom_call" | custom-call | flops 7927234560 | bytes 49545216 | tf_op jit(solution)/shard_map/moe_step/pallas_call | solution.py:367
  77.3 1.6 %copy.10 = bf16[128,768]{1,0:T(8,128)(2,1)} copy(bf16[128,768]{1,0:T(8,128)(2,1)} %moe_step.1) | data formatting | bytes 393216

commit v2 on v1

--- a/solution.py
+++ b/solution.py
@@ -67,7 +67,7 @@
 
 
 def kernel(cfg, tok_h, rou_h, gat_h, wg_h, wu_h, wd_h, out_ref,
-           tok, rou, gat, wg, wu, wd, sbuf, xr, xa, xb, xc, hid, carry, acc, pbuf, ret, wmat,
+           tok, rou, gat, flip, wg, wu, wd, sbuf, xr, xa, xb, xc, hid, turn, carry, acc, pbuf, ret, wmat,
            in_sem, w_sem, d_sem, ds_send, ds_recv, fw_send, fw_recv,
            up_send, dn_send, sb_send, ag_recv, rt_send, rt_recv):
     depth, units, feats, rows = cfg
@@ -125,14 +125,18 @@
     named = jnp.where(group == 0, rel[0], jnp.where(group == 1, rel[1], jnp.where(group == 2, rel[2], rel[3])))
     named = jnp.where(lane >= 4 * CAP, -1, named)
     slot = lane - CAP * group
-    routes = rou[...]
-    gates = gat[...]
+    top = rou.shape[0]
+    flip[...] = jnp.zeros_like(flip)
+    flip[0:top, :] = rou[...].astype(jnp.float32)
+    flip[top:2 * top, :] = gat[...]
+    columns = flip[...].T
+    named = named.astype(jnp.float32)
     chosen = jnp.zeros((rows, 256), jnp.float32)
     weight = jnp.zeros((rows, 256), jnp.float32)
-    for k in range(routes.shape[1]):
-        hit = routes[:, k:k + 1] == named
+    for k in range(top):
+        hit = columns[:, k:k + 1] == named
         chosen = jnp.where(hit, 1.0, chosen)
-        weight = jnp.where(hit, gates[:, k:k + 1], weight)
+        weight = jnp.where(hit, columns[:, top + k:top + k + 1], weight)
     lower = (lax.broadcasted_iota(jnp.int32, (rows, rows), 0) >= lax.broadcasted_iota(jnp.int32, (rows, rows), 1))
     lower = jnp.where(lower, 1.0, 0.0).astype(jnp.bfloat16)
     count = jnp.dot(lower, chosen.astype(jnp.bfloat16), preferred_element_type=jnp.float32)
@@ -144,8 +148,6 @@
     pick = match.T.astype(jnp.bfloat16)[:4 * CAP]
 
     small[2].wait()
-    for r in (1, 2, 3):
-        pass
     for piece in range(0, quarter, 512):
         vals = []
         for q in range(2):
@@ -236,15 +238,17 @@
 
     def compute(p, g):
         start, size = groups[g]
-        for col in range(start, start + size, CHUNK):
-            width = min(CHUNK, start + size - col)
+        step = CHUNK if p == 0 else 512
+        for col in range(start, start + size, step):
+            width = min(step, start + size - col)
             if p == 0:
                 for copy in loads[col // CHUNK]:
                     copy.wait()
-            left = xs[p][...]
-            ga = contract_last(left, wg[col:col + width, :])
-            ua = contract_last(left, wu[col:col + width, :])
-            h = ga / (1.0 + jnp.exp(-ga)) * ua
+            few = xs[p][...]
+            ga = contract_last(wg[col:col + width, :], few)
+            ua = contract_last(wu[col:col + width, :], few)
+            turn[:width, :few.shape[0]] = ga / (1.0 + jnp.exp(-ga)) * ua
+            h = turn[:width, :].T
             if p == 0:
                 full = h[:32]
                 carry[0, :, col:col + width] = h[32:40]
@@ -300,11 +304,11 @@
                     hop(shard, n, sb_send.at[0, 0, n], sib).wait_recv()
             off = pl.multiple_of(src * 2 * units + q * (units - half_pad), 128)
             for col in range(0, feats, CHUNK):
-                part = contract_last(hid[shard], wd[col:col + CHUNK, pl.ds(off, pad_units)])
+                part = contract_last(wd[col:col + CHUNK, pl.ds(off, pad_units)], hid[shard])
                 if first and q == 0:
-                    acc[:, col:col + CHUNK] = part
+                    acc[col:col + CHUNK, :4 * CAP] = part
                 else:
-                    acc[:, col:col + CHUNK] += part
+                    acc[col:col + CHUNK, :4 * CAP] += part
 
     wd_load.wait()
     down(z, True)
@@ -317,8 +321,9 @@
 
     half_f = feats // 2
     back = []
+    sums = acc[...].T
     for r in (3, 1, 2, 0):
-        block = acc[r * CAP:(r + 1) * CAP, :]
+        block = sums[r * CAP:(r + 1) * CAP, :]
         packed = jnp.concatenate([block[:, :half_f], block[:, half_f:]], axis=0).astype(jnp.bfloat16)
         if r == 0:
             ret[0] = packed
@@ -371,8 +376,9 @@
         out_specs=pl.BlockSpec(memory_space=pltpu.VMEM),
         scratch_shapes=[
             pltpu.VMEM((rows, depth), bf),
-            pltpu.VMEM(routes.shape, jnp.int32),
-            pltpu.VMEM(gates.shape, jnp.float32),
+            pltpu.VMEM(routes.shape[::-1], jnp.int32),
+            pltpu.VMEM(gates.shape[::-1], jnp.float32),
+            pltpu.VMEM((128, rows), jnp.float32),
             pltpu.VMEM((pad_units, depth), bf),
             pltpu.VMEM((pad_units, depth), bf),
             pltpu.VMEM((feats, down_proj.shape[2]), bf),
@@ -382,8 +388,9 @@
             pltpu.VMEM((80, depth), bf),
             pltpu.VMEM((48, depth), bf),
             pltpu.VMEM((8, 4 * CAP, pad_units), bf),
+            pltpu.VMEM((512, 128), jnp.float32),
             pltpu.VMEM((2, 8, pad_units), jnp.float32),
-            pltpu.VMEM((4 * CAP, feats), jnp.float32),
+            pltpu.VMEM((feats, 256), jnp.float32),
             pltpu.VMEM((3, 2 * CAP, feats // 2), bf),
             pltpu.VMEM((4, 2 * CAP, feats // 2), bf),
             pltpu.VMEM((2, rows, 256), bf),
@@ -398,7 +405,7 @@
             flops=2 * 4 * CAP * 3 * units * depth, transcendentals=4 * CAP * units,
             bytes_accessed=3 * 2 * units * depth),
         name="moe_step",
-    )(tokens, routes, gates, gate_proj, up_proj, down_proj)
+    )(tokens, routes.T, gates.T, gate_proj, up_proj, down_proj)
 
 
 def tiles(mesh):

time: 79.1 us -> 73 us (0.923)
  Pallas kernels: 74.5 us -> 71.3 us
  local copies, waits for them, and re-layouts: 4.44 us -> 1.62 us
    pallas_call x1, Pallas kernels: 74.5 us -> 71.3 us  [fast_body(): pl.pallas_call(functools.partial(kernel, (depth, units, feats, rows)), ou...]
    unnamed x3 -> x1, local copies, waits for them, and re-layouts: 4.44 us -> 1.62 us
where the time goes in v2:
time: 73 us; the launch traced here: 72.9 us
  Pallas kernels  71.3 us (98%)
  local copies, waits for them, and re-layouts  1.62 us (2%)
    pallas_call x1, Pallas kernels, fast_body(): pl.pallas_call(functools.partial(kernel, (depth, units, feats, rows)), ou...  71.3 us
    unnamed x1, local copies, waits for them, and re-layouts  1.62 us

profile of v2, /device:TPU:0, one launch (start us, length us, event | category | flops | bytes accessed | tf_op | source)
XLA Modules:
  0.0 72.9 jit_solution(2224481697487860693)
XLA Ops:
  0.0 71.3 %moe_step.1 = bf16[128,768]{1,0:T(8,128)(2,1)} custom-call(bf16[128,6144]{1,0:T(8,128)(2,1)} %tok_h.1, s32[4,128]{1,0:T(4,128)} %bitcast.2, f32[4,128]{1,0:T(4,128)} %bitcast.3, bf16[1,1344,6144]{2,1,0:T(8,128)(2,1)} %wg_h.1, bf16[1,1344,6144]{2,1,0:T(8,128)(2,1)} %wu_h.1, bf16[1,768,10752]{2,1,0:T(8,128)(2,1)} %wd_h.1), custom_call_target="tpu_custom_call" | custom-call | flops 7927234560 | bytes 49545216 | tf_op jit(solution)/shard_map/moe_step/pallas_call | solution.py:372
  71.3 1.6 %copy.8 = bf16[128,768]{1,0:T(8,128)(2,1)} copy(bf16[128,768]{1,0:T(8,128)(2,1)} %moe_step.1) | data formatting | bytes 393216

commit v3 on v2

--- a/solution.py
+++ b/solution.py
@@ -117,6 +117,8 @@
     @pl.when(z > 0)
     def _():
         pl.semaphore_signal(barrier, inc=1, device_id=(me, t - 2), device_id_type=MESH)
+
+    pl.semaphore_signal(barrier, inc=1, device_id=(me, (t + 4) % 8), device_id_type=MESH)
 
     small[0].wait()
     small[1].wait()
@@ -156,13 +158,14 @@
         for r in (1, 2, 3):
             both = jnp.concatenate([v[r * CAP:(r + 1) * CAP] for v in vals], axis=0)
             sbuf[r - 1, :, piece:piece + 512] = both.astype(jnp.bfloat16)
-    pl.semaphore_wait(barrier, 4 + (z > 0).astype(jnp.int32) + (z < chips - 1).astype(jnp.int32))
+    pl.semaphore_wait(barrier, 5 + (z > 0).astype(jnp.int32) + (z < chips - 1).astype(jnp.int32))
     sends = []
     for r in (1, 2, 3):
         copy = pltpu.make_async_remote_copy(
             src_ref=sbuf.at[r - 1], dst_ref=xr.at[c, r - 1], send_sem=ds_send.at[r - 1],
             recv_sem=ds_recv.at[r - 1], device_id=(rel[r], t), device_id_type=MESH)
-        copy.start()
+        if r < 3:
+            copy.start()
         sends.append(copy)
     own = jnp.concatenate([pick[:CAP].astype(jnp.float32), jnp.zeros((8, rows), jnp.float32)], axis=0).astype(jnp.bfloat16)
     for col in range(0, depth, 512):
@@ -199,40 +202,29 @@
             src_ref=window(shard, n), dst_ref=window(shard, n), send_sem=sem,
             recv_sem=ag_recv.at[shard, n], device_id=(me, dev), device_id_type=MESH)
 
-    def push(shard, dist, n, do_up, do_dn):
-        if do_up:
-            @pl.when(z < chips - 1)
+    def own_hops(n):
+        return ((z < 2, hop(t, n, up_send.at[1, n], t + 4)), (z >= 2, hop(t, n, dn_send.at[1, n], t - 4)),
+                (z < 3, hop(t, n, up_send.at[0, n], t + 2)), (z > 0, hop(t, n, dn_send.at[0, n], t - 2)))
+
+    def relay_hops(n):
+        return ((z == 2, hop(t - 4, n, up_send.at[2, n], t + 2)), (z == 1, hop(t + 4, n, dn_send.at[2, n], t - 2)))
+
+    def start_all(hops):
+        for cond, copy in hops:
+            pl.when(cond)(copy.start)
+
+    def drain_all(hops):
+        for cond, copy in hops:
+            pl.when(cond)(copy.wait_send)
+
+    def take(dist, n):
+        for side, cond, shard in ((0, z >= dist, t - 2 * dist), (1, z + dist <= chips - 1, t + 2 * dist)):
+            @pl.when(cond)
             def _():
-                hop(shard, n, up_send.at[dist, n], t + 2).start()
-        if do_dn:
-            @pl.when(z > 0)
-            def _():
-                hop(shard, n, dn_send.at[dist, n], t - 2).start()
-
-    def drain(shard, dist, n, do_up, do_dn):
-        if do_up:
-            @pl.when(z < chips - 1)
-            def _():
-                hop(shard, n, up_send.at[dist, n], t + 2).wait_send()
-        if do_dn:
-            @pl.when(z > 0)
-            def _():
-                hop(shard, n, dn_send.at[dist, n], t - 2).wait_send()
-
-    def relay(dist, n):
-        @pl.when(z >= dist)
-        def _():
-            shard = t - 2 * dist
-            hop(shard, n, up_send.at[dist, n], t).wait_recv()
-            push(shard, dist, n, dist < chips - 1, False)
-            hop(shard, n, sb_send.at[0, dist, n], sib).start()
-
-        @pl.when(z + dist <= chips - 1)
-        def _():
-            shard = t + 2 * dist
-            hop(shard, n, dn_send.at[dist, n], t).wait_recv()
-            push(shard, dist, n, False, dist < chips - 1)
-            hop(shard, n, sb_send.at[1, dist, n], sib).start()
+                hop(shard, n, sb_send.at[side, dist, n], sib).wait_recv()
+                if dist == 2:
+                    start_all(relay_hops(n)[side:side + 1])
+                hop(shard, n, sb_send.at[side, dist, n], sib).start()
 
     xs = (xa, xb, xc)
 
@@ -280,16 +272,18 @@
                             both = jnp.concatenate([unpack(half, q, 3, piece), jnp.zeros((8, 512), jnp.float32)], axis=0)
                             xc[:, col:col + 512] = both.astype(jnp.bfloat16)
             compute(p, g)
-            push(t, 0, n, True, True)
+            start_all(own_hops(n))
             hop(t, n, sb_send.at[0, 0, n], sib).start()
-            if (p, g) == (0, 2):
+            if n == 0:
+                sends[2].start()
+            if n == 1:
                 forward(1)
                 forward(2)
-            if (p, g) == (1, 1):
+            if n == 3:
                 forward(3)
-        for dist in (1, 2, 3):
-            if 0 <= n - dist < n_pieces:
-                relay(dist, n - dist)
+        for dist, lag in ((2, 2), (1, 2), (3, 4)):
+            if n - lag >= 0:
+                take(dist, n - lag)
 
     for n in range(n_pieces):
         stage(n)
@@ -313,8 +307,10 @@
     wd_load.wait()
     down(z, True)
     low = 1 - z // 2
+    rest = ([(2, 7), (1, 7), (3, 5), (2, 8), (1, 8)], [(3, 6), (3, 7)], [(3, 8)])
     for k in (1, 2, 3):
-        stage(n_pieces + k - 1)
+        for dist, n in rest[k - 1]:
+            take(dist, n)
         up_src = k - (k <= z).astype(jnp.int32)
         dn_src = 3 - (k - (k <= 3 - z).astype(jnp.int32))
         down(low * up_src + (1 - low) * dn_src, False)
@@ -337,18 +333,12 @@
     for copy in sends + forwards:
         copy.wait_send()
     for n in range(n_pieces):
-        drain(t, 0, n, True, True)
+        drain_all(own_hops(n))
+        drain_all(relay_hops(n))
         hop(t, n, sb_send.at[0, 0, n], sib).wait_send()
         for dist in (1, 2, 3):
-            @pl.when(z >= dist)
-            def _():
-                drain(t - 2 * dist, dist, n, dist < chips - 1, False)
-                hop(t - 2 * dist, n, sb_send.at[0, dist, n], sib).wait_send()
-
-            @pl.when(z + dist <= chips - 1)
-            def _():
-                drain(t + 2 * dist, dist, n, False, dist < chips - 1)
-                hop(t + 2 * dist, n, sb_send.at[1, dist, n], sib).wait_send()
+            drain_all(((z >= dist, hop(t - 2 * dist, n, sb_send.at[0, dist, n], sib)),
+                       (z + dist <= chips - 1, hop(t + 2 * dist, n, sb_send.at[1, dist, n], sib))))
     for copy in back:
         copy.wait()
     blocks = [ret[r].astype(jnp.float32) for r in range(4)]

time: 73 us -> 70.9 us (0.971)
  Pallas kernels: 71.3 us -> 69.1 us
    pallas_call x1, Pallas kernels: 71.3 us -> 69.1 us  [fast_body(): pl.pallas_call(functools.partial(kernel, (depth, units, feats, rows)), ou...]
where the time goes in v3:
time: 70.9 us; the launch traced here: 70.7 us
  Pallas kernels  69.1 us (97%)
  local copies, waits for them, and re-layouts  1.62 us (2%)
    pallas_call x1, Pallas kernels, fast_body(): pl.pallas_call(functools.partial(kernel, (depth, units, feats, rows)), ou...  69.1 us
    unnamed x1, local copies, waits for them, and re-layouts  1.62 us

profile of v3, /device:TPU:0, one launch (start us, length us, event | category | flops | bytes accessed | tf_op | source)
XLA Modules:
  0.0 70.7 jit_solution(6275029234341330255)
XLA Ops:
  0.0 69.1 %moe_step.1 = bf16[128,768]{1,0:T(8,128)(2,1)} custom-call(bf16[128,6144]{1,0:T(8,128)(2,1)} %tok_h.1, s32[4,128]{1,0:T(4,128)} %bitcast.2, f32[4,128]{1,0:T(4,128)} %bitcast.3, bf16[1,1344,6144]{2,1,0:T(8,128)(2,1)} %wg_h.1, bf16[1,1344,6144]{2,1,0:T(8,128)(2,1)} %wu_h.1, bf16[1,768,10752]{2,1,0:T(8,128)(2,1)} %wd_h.1), custom_call_target="tpu_custom_call" | custom-call | flops 7927234560 | bytes 49545216 | tf_op jit(solution)/shard_map/moe_step/pallas_call | solution.py:362
  69.1 1.6 %copy.8 = bf16[128,768]{1,0:T(8,128)(2,1)} copy(bf16[128,768]{1,0:T(8,128)(2,1)} %moe_step.1) | data formatting | bytes 393216
